TPU v7x, 256 devices: a whole 4x4x8 slice. The times are simulated.
256 devices in a mesh: req: 8 (over y, core), ep: 32 (over x, z).
Axes of the slice: x: 4, y: 4, z: 8, core: 2. Of those that a mesh axis runs over, the one named last changes fastest.
Arguments:
- queries: bfloat16 [2048, 64, 576], P(('req', 'ep')), may hold values from -7 to 7
- latent_cache: bfloat16 [256, 512, 576], P(('req', 'ep')), may hold values from -3 to 3
- new_latents: bfloat16 [2048, 576], P(('req', 'ep')), may hold values from -4 to 4
- parents: int32 [128, 16], replicated, may hold values from 0 to 14, as said below
- cache_len: int32 [128], replicated, may hold values from 128 to 1024
- tokens: bfloat16 [2048, 7168], P(('req', 'ep')), may hold values from -6 to 6
- route_ids: int32 [2048, 8], P(('req', 'ep')), may hold values from 0 to 31, all different within a row; in each aligned block of 8 rows (0 to 7, 8 to 15, ...) at most 3 rows name the same one
- route_scores: float32 [2048, 8], P(('req', 'ep')), may hold values from 0.05 to 1
- w_gate: bfloat16 [32, 7168, 2048], P('ep', None, 'req'), may hold values from -0.0625 to 0.0625
- w_up: bfloat16 [32, 7168, 2048], P('ep', None, 'req'), may hold values from -0.0625 to 0.0625
- w_down: bfloat16 [32, 2048, 7168], P('ep', 'req'), may hold values from -0.125 to 0.125
Outputs:
- attention_out: bfloat16 [2048, 64, 512], P(('req', 'ep'))
- moe_out: bfloat16 [2048, 7168], P(('req', 'ep'))
Inputs may be any that keep to these rules, and one draw needn't show every extreme that they name: `route_ids`: each row names 8 different experts. Among the 8 tokens of one device (aligned blocks of 8 rows) no expert is named by more than 3 tokens, a bound that some block reaches. parents[q, 0] = 0 and parents[q, j] < j for j >= 1.
All inputs are finite; a program needn't handle non-finite values.
Results may differ from a plain program's by a relative error of at most 0.015.
Values may be sent and summed in bfloat16 or wider, within the bound.
A program may use at most 128 MiB of HBM per device.

v0:
```python
import jax
import jax.numpy as jnp
from jax import lax
from jax.sharding import PartitionSpec as P

VDIM = 512


score_scale = 192.0 ** (-0.5)
route_scale = 2.5


def partner(block, axis, stride):
    count = lax.axis_size(axis)
    route = []
    for low in range(count):
        high = low | 1 << stride
        if high != low and high < count:
            route += [(low, high), (high, low)]
    return lax.ppermute(block, axis, route)


def ancestor_table(parent_row):
    node_count = parent_row.shape[0]
    node_ids = jnp.arange(node_count, dtype=jnp.int32)
    current = node_ids
    visible = node_ids[:, None] == node_ids[None, :]
    for repeat in range(node_count):
        current = parent_row[current]
        visible = visible | (current[:, None] == node_ids[None, :])
    return visible


def expert_mlp(row_block, w_gate, w_up, w_down):
    gate_val = jnp.dot(row_block, w_gate[0], preferred_element_type=jnp.float32)
    up_val = jnp.dot(row_block, w_up[0], preferred_element_type=jnp.float32)
    hidden = (jax.nn.silu(gate_val) * up_val).astype(jnp.bfloat16)
    return jnp.dot(hidden, w_down[0], preferred_element_type=jnp.float32).astype(jnp.bfloat16)


def body(
    queries,
    latent_cache,
    new_latents,
    parents,
    cache_len,
    tokens,
    route_ids,
    route_scores,
    w_gate,
    w_up,
    w_down,
):
    ep_count = lax.axis_size("ep")
    position = lax.axis_index("req") * ep_count + lax.axis_index("ep")
    request = position // 2
    half_index = position % 2
    tok_dev = tokens.shape[0]
    model_width = tokens.shape[1]
    other_cache, other_fresh = partner((latent_cache, new_latents), "ep", 0)
    lower_half = half_index == 0
    cache_rows = jnp.concatenate(
        [
            jnp.where(lower_half, latent_cache[0], other_cache[0]),
            jnp.where(lower_half, other_cache[0], latent_cache[0]),
        ],
        axis=0,
    )
    fresh_rows = jnp.concatenate(
        [
            jnp.where(lower_half, new_latents, other_fresh),
            jnp.where(lower_half, other_fresh, new_latents),
        ],
        axis=0,
    )
    key_rows = jnp.concatenate([cache_rows, fresh_rows], axis=0)
    context = cache_rows.shape[0]
    parent_row = lax.dynamic_index_in_dim(parents, request, 0, keepdims=False)
    tree_vis = lax.dynamic_slice_in_dim(
        ancestor_table(parent_row), half_index * tok_dev, tok_dev, 0
    )
    length = lax.dynamic_index_in_dim(cache_len, request, 0, keepdims=False)
    cached = jnp.arange(context, dtype=jnp.int32) < length
    visible = jnp.concatenate(
        [jnp.broadcast_to(cached[None, :], (tok_dev, context)), tree_vis], axis=1
    )
    head_count = queries.shape[1]
    flat_query = queries.reshape(tok_dev * head_count, queries.shape[2])
    scores = (
        lax.dot_general(
            flat_query, key_rows, (((1,), (1,)), ((), ())), preferred_element_type=jnp.float32
        )
        * score_scale
    )
    scores = scores.reshape(tok_dev, head_count, key_rows.shape[0])
    masked = jnp.where(visible[:, None, :], scores, -jnp.inf)
    row_max = jnp.max(masked, axis=-1, keepdims=True)
    shifted = jnp.exp(masked - row_max)
    attn_probs = (shifted / jnp.sum(shifted, axis=-1, keepdims=True)).astype(jnp.bfloat16)
    value_rows = key_rows[:, :VDIM]
    attended = jnp.dot(
        attn_probs.reshape(tok_dev * head_count, key_rows.shape[0]),
        value_rows,
        preferred_element_type=jnp.float32,
    )
    attention_out = attended.reshape(tok_dev, head_count, VDIM).astype(jnp.bfloat16)
    top_count = route_ids.shape[1]
    capacity = min(tok_dev, tok_dev * top_count // ep_count + 1)
    route_weight = route_scale * route_scores / jnp.sum(route_scores, axis=1, keepdims=True)
    pair_ids = route_ids.reshape(-1)
    onehot = (pair_ids[:, None] == jnp.arange(ep_count, dtype=jnp.int32)[None, :]).astype(jnp.int32)
    slot_rank = jnp.sum(jnp.cumsum(onehot, axis=0) * onehot, axis=1) - 1
    slot_of = (pair_ids * capacity + slot_rank).reshape(tok_dev, top_count)
    slot_ids = jnp.arange(ep_count * capacity, dtype=jnp.int32)
    slot_hits = slot_of[None, :, :] == slot_ids[:, None, None]
    dispatch = jnp.any(slot_hits, axis=2).astype(jnp.bfloat16)
    combine = jnp.sum(jnp.where(slot_hits, route_weight[None, :, :], 0.0), axis=2)
    outgoing = jnp.dot(dispatch, tokens, preferred_element_type=jnp.float32).astype(jnp.bfloat16)
    outgoing = outgoing.reshape(ep_count, capacity, model_width)
    arrived = lax.all_to_all(outgoing, "ep", split_axis=0, concat_axis=0, tiled=True)
    partial_value = expert_mlp(
        lax.all_gather(
            arrived.reshape(ep_count * capacity, model_width), "req", axis=0, tiled=True
        ),
        w_gate,
        w_up,
        w_down,
    )
    summed = lax.psum_scatter(
        partial_value.astype(jnp.float32).astype(jnp.bfloat16),
        "req",
        scatter_dimension=0,
        tiled=True,
    ).astype(jnp.float32)
    summed = summed.reshape(ep_count, capacity, model_width)
    returned = lax.all_to_all(
        summed.astype(jnp.bfloat16), "ep", split_axis=0, concat_axis=0, tiled=True
    ).astype(summed.dtype)
    moe_out = lax.dot_general(
        combine,
        returned.reshape(ep_count * capacity, model_width),
        (((0,), (0,)), ((), ())),
        precision=lax.Precision.HIGHEST,
        preferred_element_type=jnp.float32,
    )
    return (attention_out, moe_out.astype(jnp.bfloat16))


def solution(mesh):
    placed = (
        P(("req", "ep"), None, None),
        P(("req", "ep"), None, None),
        P(("req", "ep"), None),
        P(),
        P(),
        P(("req", "ep"), None),
        P(("req", "ep"), None),
        P(("req", "ep"), None),
        P("ep", None, "req"),
        P("ep", None, "req"),
        P("ep", "req", None),
    )
    return jax.shard_map(
        body,
        mesh=mesh,
        in_specs=placed,
        out_specs=(P(("req", "ep"), None, None), P(("req", "ep"), None)),
        check_vma=False,
    )
```

profile of v0, /device:TPU:1, one launch (start us, length us, event | category | flops | bytes accessed | tf_op | source)
XLA Modules:
  0.0 298.0 jit_solution(5161164357514581001)
XLA Ops:
  7.2 0.8 eq.306
  8.5 0.7 multiply_add_fusion
  9.3 2.5 convolution_convert_fusion.1
  11.8 2.6 reshape.271
  14.5 53.2 %all_to_all.10 = bf16[32,3,7168]{2,1,0:T(4,128)(2,1)} all-to-all(bf16[32,3,7168]{2,1,0:T(4,128)(2,1)S(1)} %reshape.271), channel_id=1, replica_groups=mesh['req'=8,'ep'=32] {'ep'}, dimensions={0} | all-to-all | bytes 2752512 | tf_op jit(solution)/shard_map/all_to_all | solution.py:120
  67.7 4.1 %reshape.272 = bf16[96,7168]{1,0:T(8,128)(2,1)} reshape(bf16[32,3,7168]{2,1,0:T(4,128)(2,1)} %all_to_all.10) | data formatting | bytes 2752512 | tf_op jit(solution)/shard_map/reshape | solution.py:123
  71.9 64.9 %all-gather.2.cloned.1.call-done = bf16[768,7168]{1,0:T(8,128)(2,1)} async-done(((bf16[96,7168]{1,0:T(8,128)(2,1)}), bf16[768,7168]{1,0:T(8,128)(2,1)}) %all-gather.2.cloned.1.call-update) | async-done | bytes 11010064 | tf_op jit(solution)/shard_map/all_gather | solution.py:122
  136.8 6.9 %fusion.3 = f32[768,256]{1,0:T(8,128)S(1)} fusion(bf16[768,7168]{1,0:T(8,128)(2,1)} %all-gather.2.cloned.1.call-done, bf16[1,7168,256]{2,1,0:T(8,128)(2,1)} %param.19), kind=kOutput, calls=%fused_computation.22 | convolution fusion | flops 2818572288 | bytes 15466496 | tf_op jit(solution)/shard_map/dot_general | solution.py:35
  143.7 18.9 %convolution_convert_fusion = bf16[768,7168]{1,0:T(8,128)(2,1)} fusion(bf16[1,256,7168]{2,1,0:T(8,128)(2,1)} %param.21, bf16[768,7168]{1,0:T(8,128)(2,1)} %all-gather.2.cloned.1.call-done, bf16[1,7168,256]{2,1,0:T(8,128)(2,1)} %param.20, f32[768,256]{1,0:T(8,128)S(1)} %fusion.3), kind=kOutput, calls=%fused_computation.16 | convolution fusion | flops 5643829248 | bytes 30146560 | tf_op jit(solution)/shard_map/dot_general | solution.py:38
  162.6 1.4 collective-permute-start
  165.5 0.7 gather_fusion.1
  166.1 0.7 gather_fusion.2
  166.8 0.7 gather_fusion.3
  167.5 0.7 gather_fusion.4
  168.2 0.7 gather_fusion.5
  168.9 0.7 gather_fusion.6
  169.5 0.7 gather_fusion.7
  177.5 52.1 %reduce-scatter.2.cloned.1.call-done = bf16[96,7168]{1,0:T(8,128)(2,1)} async-done(((bf16[768,7168]{1,0:T(8,128)(2,1)}), bf16[96,7168]{1,0:T(8,128)(2,1)}) %reduce-scatter.2.cloned.1.call-update) | async-done | bytes 1376272 | tf_op jit(solution)/shard_map/reduce_scatter | solution.py:129
  229.6 4.0 %convert_element_type.37 = bf16[32,3,7168]{2,1,0:T(4,128)(2,1)} reshape(bf16[96,7168]{1,0:T(8,128)(2,1)} %reduce-scatter.2.cloned.1.call-done) | data formatting | bytes 2752512 | tf_op jit(solution)/shard_map/convert_element_type | solution.py:137
  233.6 9.8 %all-to-all-start.1 = ((bf16[32,3,7168]{2,1,0:T(4,128)(2,1)}), bf16[32,3,7168]{2,1,0:T(4,128)(2,1)S(1)}, u32[]{:S(2)}, u32[]{:S(2)}) async-start(bf16[32,3,7168]{2,1,0:T(4,128)(2,1)} %convert_element_type.37), calls=%async_computation.2 | async-start | bytes 3670016 | tf_op jit(solution)/shard_map/all_to_all | solution.py:136
  243.6 0.7 select_reduce_fusion
  244.3 1.4 copy.28
  245.6 1.0 broadcast_in_dim.21
  246.6 2.4 copy.32
  249.1 2.2 copy.29
  251.2 1.3 select_bitcast_fusion.1
  252.6 1.2 fusion.70
  254.5 1.4 copy.33
  255.9 3.2 %convolution_convert_fusion.3 = bf16[8,64,512]{2,1,0:T(8,128)(2,1)} fusion(bf16[8,64,1040]{2,1,0:T(8,128)(2,1)} %bitcast.100, bf16[8,576]{1,0:T(8,128)(2,1)} %copy-done.8, bf16[8,576]{1,0:T(8,128)(2,1)} %copy-done.7, bf16[512,576]{1,0:T(8,128)(2,1)} %copy-done.2, bf16[512,576]{1,0:T(8,128)(2,1)} %copy-done.1), kind=kOutput, calls=%fused_computation.37 | convolution fusion | flops 549781504 | bytes 2787328 | tf_op jit(solution)/shard_map/dot_general | solution.py:101
  259.1 27.1 %all-to-all-done.1 = bf16[32,3,7168]{2,1,0:T(4,128)(2,1)S(1)} async-done(((bf16[32,3,7168]{2,1,0:T(4,128)(2,1)}), bf16[32,3,7168]{2,1,0:T(4,128)(2,1)S(1)}, u32[]{:S(2)}, u32[]{:S(2)}) %all-to-all-start.1) | async-done | bytes 1376288 | tf_op jit(solution)/shard_map/all_to_all | solution.py:136
  286.2 2.4 reshape.273
  288.6 2.6 convolution_convert_fusion.2
  (93 shorter events, 10.4 us)
Async XLA Ops:
  7.2 245.4 %copy-start = (bf16[8,64,576]{2,1,0:T(8,128)(2,1)S(1)}, bf16[8,64,576]{2,1,0:T(8,128)(2,1)}, u32[]{:S(2)}) copy-start(bf16[8,64,576]{2,1,0:T(8,128)(2,1)} %param.11) | copy-start | bytes 1769476
  7.2 129.6 %all-gather.2.cloned.1.call-start = ((), (), s32[]{:S(2)}) async-start(), calls=%async_computation.3 | async-start | bytes 12386304 | tf_op jit(solution)/shard_map/all_gather | solution.py:122
  71.9 157.7 %reduce-scatter.2.cloned.1.call-start = ((), (), s32[]{:S(2)}) async-start(), calls=%async_computation.4 | async-start | bytes 12386304 | tf_op jit(solution)/shard_map/reduce_scatter | solution.py:129
  162.6 1.4 copy-start.6
  162.6 2.0 copy-start.9
  162.6 86.5 %collective-permute-start = (bf16[1,512,576]{1,2,0:T(8,128)(2,1)}, bf16[1,512,576]{1,2,0:T(8,128)(2,1)}, u32[]{:S(2)}, u32[]{:S(2)}) collective-permute-start(bf16[1,512,576]{1,2,0:T(8,128)(2,1)} %param.12), channel_id=1, source_target_pairs={{0,1},{1,0},{2,3},{3,2},{4,5},{5,4},{6,7},{7,6},{8,9},{9,8},{10,11... | collective-permute-start | bytes 1769480 | tf_op jit(solution)/shard_map/ppermute | solution.py:20
  164.0 85.1 %collective-permute-start.1 = (bf16[8,576]{1,0:T(8,128)(2,1)S(1)}, bf16[8,576]{1,0:T(8,128)(2,1)S(1)}, u32[]{:S(2)}, u32[]{:S(2)}) collective-permute-start(bf16[8,576]{1,0:T(8,128)(2,1)S(1)} %copy-done.6), channel_id=1, source_target_pairs={{0,1},{1,0},{2,3},{3,2},{4,5},{5,4},{6,7},{7,6},{8,9},{9,8},{10,11... | collective-permute-start | bytes 27656 | tf_op jit(solution)/shard_map/ppermute | solution.py:20
  170.2 5.8 %copy-start.10 = (s32[128]{0:T(128)S(1)}, s32[128]{0:T(128)}, u32[]{:S(2)}) copy-start(s32[128]{0:T(128)} %param.15) | copy-start | bytes 1540
  233.6 9.8 %copy-start.5 = (f32[8,8]{1,0:T(8,128)S(1)}, f32[8,8]{1,0:T(8,128)}, u32[]{:S(2)}) copy-start(f32[8,8]{1,0:T(8,128)} %param.18) | copy-start | bytes 772
  233.6 52.6 %all-to-all-start.1 = ((bf16[32,3,7168]{2,1,0:T(4,128)(2,1)}), bf16[32,3,7168]{2,1,0:T(4,128)(2,1)S(1)}, u32[]{:S(2)}, u32[]{:S(2)}) async-start(bf16[32,3,7168]{2,1,0:T(4,128)(2,1)} %convert_element_type.37), calls=%async_computation.2 | async-start | bytes 3670016 | tf_op jit(solution)/shard_map/all_to_all | solution.py:136
  249.1 4.7 %copy-start.7 = (bf16[8,576]{1,0:T(8,128)(2,1)}, bf16[8,576]{1,0:T(8,128)(2,1)S(1)}, u32[]{:S(2)}) copy-start(bf16[8,576]{1,0:T(8,128)(2,1)S(1)} %get-tuple-element.4) | copy-start | bytes 27652
  249.1 4.7 %copy-start.8 = (bf16[8,576]{1,0:T(8,128)(2,1)}, bf16[8,576]{1,0:T(8,128)(2,1)S(1)}, u32[]{:S(2)}) copy-start(bf16[8,576]{1,0:T(8,128)(2,1)S(1)} %get-tuple-element.5) | copy-start | bytes 27652
  251.2 1.3 copy-start.3
  252.5 1.2 copy-start.1
  252.5 1.2 copy-start.2
  259.1 29.4 %copy-start.4 = (f32[96,8]{0,1:T(8,128)S(1)}, f32[96,8]{0,1:T(8,128)}, u32[]{:S(2)}) copy-start(f32[96,8]{0,1:T(8,128)} %select_reduce_fusion) | copy-start | bytes 9220
Sparse Core Ops, SparseCore 0:
  72.0 64.7 all-gather.1
  162.7 66.8 reduce-scatter.1
where the time goes:
time: 300 us; the launch traced here: 298 us
  waiting for transfers between devices  144 us (48%)
  blocking collectives  53.2 us (18%)
  matrix products  35.4 us (12%)
  local copies, waits for them, and re-layouts  34.1 us (11%)
  between operations  14.4 us (5%)
  starting transfers between devices  11.8 us (4%)
  other arithmetic  5.09 us (2%)
    all_gather x1, waiting for transfers between devices, body(): lax.all_gather(arrived.reshape(ep_count * capacity, model_width), 'req',...  64.9 us
    all_to_all x1, blocking collectives, body(): lax.all_to_all(outgoing, 'ep', split_axis=0, concat_axis=0, tiled=True)  53.2 us
    reduce_scatter x1, waiting for transfers between devices, body(): lax.psum_scatter(partial_value.astype(jnp.float32).astype(jnp.bfloat16),...  52.1 us
    all_to_all x1, waiting for transfers between devices, body(): lax.all_to_all(summed.astype(jnp.bfloat16), 'ep', split_axis=0, concat_ax...  27.1 us
    dot_general x1, matrix products, expert_mlp(): jnp.dot(hidden, w_down[0], preferred_element_type=jnp.float32)  18.9 us
    gather x16, local copies, waits for them, and re-layouts, ancestor_table(): current = parent_row[current]  10.5 us
    all_to_all x1, starting transfers between devices, body(): lax.all_to_all(summed.astype(jnp.bfloat16), 'ep', split_axis=0, concat_ax...  9.79 us
    dot_general x1, matrix products, expert_mlp(): gate_val = jnp.dot(row_block, w_gate[0], preferred_element_type=jnp.float32)  6.88 us
  transfers between devices with their start and end apart: 5, of which 3 were waited for; matrix products, arithmetic and copies ran while one was open for 11% of the time, Pallas kernels for 0%

commit v1 on v0

v1 whole, which is shorter than its diff:
```python
import functools

import jax
import jax.numpy as jnp
from jax import lax
from jax.experimental import pallas as pl
from jax.experimental.pallas import tpu as pltpu
from jax.sharding import PartitionSpec as P

VDIM = 512
NX, NZ, NY, NC = 4, 8, 4, 2
CAP = 3
PAD = 4
CHUNKS = 7

score_scale = 192.0 ** (-0.5)
route_scale = 2.5
F32, BF16 = jnp.float32, jnp.bfloat16
MESH = pl.DeviceIdType.MESH


def iota(shape, dim):
    return lax.broadcasted_iota(jnp.int32, shape, dim)


def mm(a, b):
    return jnp.dot(a, b, preferred_element_type=F32)


def mm_nt(a, b):
    return lax.dot_general(a, b, (((1,), (1,)), ((), ())), preferred_element_type=F32)


def kernel(
    tok, rid, rsc, queries, cache, newlat, parents, clen, wg_h, wu_h, wd_h,
    attn_out, moe_out,
    wg, wu, wd, qbuf, cachebuf, fresh, vis, obuf,
    msend, metabuf, smat, pmat, emat, whi, wlo,
    zbuf, xsend, xbuf, ybuf, gacc, uacc, act,
    dsend, drecv, r1send, r1recv, r2send, r2recv, x2send, x2buf, z2send, z2buf,
    loc_sem, out_sem, c_send, c_recv, m_send, m_recv,
    z_send, z_recv, x_send, x_recv, y_send, y_recv, s_send, s_recv,
    d_send, d_recv, r1_send, r1_recv, r2_send, r2_recv, x2_send, x2_recv, z2_send, z2_recv,
):
    req, ep = lax.axis_index("req"), lax.axis_index("ep")
    my_y, my_c = req // NC, req % NC
    my_x, my_z = ep // NZ, ep % NZ
    K = CHUNKS
    T = tok.shape[0]
    C = tok.shape[1] // K
    S = NZ * PAD
    R = NX * NZ * CAP
    HR = R // 2
    FF = wg.shape[1]
    rot = lambda a, j, n: lax.rem(a + j + n, n)
    nxt, prv, far = rot(my_y, 1, NY), rot(my_y, -1, NY), rot(my_y, 2, NY)
    dev_y = lambda y: (y * NC + my_c, ep)
    dev_x = lambda x: (req, x * NZ + my_z)
    dev_z = lambda z: (req, my_x * NZ + z)
    sib = (my_y * NC + (1 - my_c), ep)
    blk_of = lambda y: my_c * NY + y
    half = ep % 2
    mate = (req, ep + 1 - 2 * half)
    cols = lambda k: pl.ds(pl.multiple_of(k * C, 128), C)

    def remote(src, dst, ssem, rsem, device):
        return pltpu.make_async_remote_copy(
            src_ref=src, dst_ref=dst, send_sem=ssem, recv_sem=rsem,
            device_id=device, device_id_type=MESH,
        )

    def meta_copy(j):
        return remote(msend, metabuf.at[my_z], m_send.at[j - 1], m_recv.at[j - 1],
                      dev_z(rot(my_z, j, NZ)))

    def z_copy(k, j):
        return remote(tok.at[:, cols(k)], zbuf.at[k, my_z], z_send.at[k, j - 1],
                      z_recv.at[k, j - 1], dev_z(rot(my_z, j, NZ)))

    def x_copy(k, j):
        to = rot(my_x, j, NX)
        return remote(xsend.at[k, to], xbuf.at[k, my_x], x_send.at[k, j - 1],
                      x_recv.at[k, j - 1], dev_x(to))

    def y_copy(k, i):
        if i < 2:
            ref = ybuf.at[k, blk_of(my_y)]
        elif i == 2:
            ref = ybuf.at[k, blk_of(prv), pl.ds(0, HR)]
        else:
            ref = ybuf.at[k, blk_of(nxt), pl.ds(HR, HR)]
        return remote(ref, ref, y_send.at[k, i], y_recv.at[k, i],
                      dev_y(nxt if i % 2 == 0 else prv))

    def s_copy(k, i):
        ref = ybuf.at[k, blk_of((my_y, prv, nxt, far)[i])]
        return remote(ref, ref, s_send.at[k, i], s_recv.at[k, i], sib)

    def d_copy(k):
        return remote(dsend.at[k], drecv.at[k], d_send.at[k], d_recv.at[k], sib)

    def r1_copy(k, i):
        return remote(r1send.at[k, i], r1recv.at[k, i], r1_send.at[k, i], r1_recv.at[k, i],
                      dev_y(nxt if i == 0 else prv))

    def r2_copy(k, i):
        return remote(r2send.at[k, i], r2recv.at[k, i], r2_send.at[k, i], r2_recv.at[k, i],
                      dev_y(nxt if i == 0 else prv))

    def x2_copy(k, j):
        to = rot(my_x, j, NX)
        return remote(x2send.at[k, to], x2buf.at[k, my_x], x2_send.at[k, j - 1],
                      x2_recv.at[k, j - 1], dev_x(to))

    def z2_copy(k, j):
        to = rot(my_z, j, NZ)
        return remote(z2send.at[k, to], z2buf.at[k, my_z], z2_send.at[k, j - 1],
                      z2_recv.at[k, j - 1], dev_z(to))

    cache_copy = remote(cache.at[0], cachebuf.at[half], c_send.at[0], c_recv.at[0], mate)
    fresh_copy = remote(newlat, fresh.at[half], c_send.at[1], c_recv.at[1], mate)
    local = [
        pltpu.make_async_copy(wg_h.at[0], wg, loc_sem.at[0]),
        pltpu.make_async_copy(wu_h.at[0], wu, loc_sem.at[1]),
        pltpu.make_async_copy(wd_h.at[0], wd, loc_sem.at[2]),
        pltpu.make_async_copy(queries, qbuf, loc_sem.at[3]),
        pltpu.make_async_copy(cache.at[0], cachebuf.at[half], loc_sem.at[4]),
    ]

    barrier = pltpu.get_barrier_semaphore()
    peers = [dev_z(rot(my_z, j, NZ)) for j in range(1, NZ)]
    peers += [dev_x(rot(my_x, j, NX)) for j in range(1, NX)]
    peers += [dev_y(nxt), dev_y(prv), sib]
    for peer in peers:
        pl.semaphore_signal(barrier, inc=1, device_id=peer, device_id_type=MESH)
    msend[...] = jnp.zeros_like(msend)
    msend[0:T, 0:rid.shape[1]] = rid[...].astype(F32)
    scores = rsc[...]
    msend[T:2 * T, 0:rid.shape[1]] = route_scale * scores / jnp.sum(scores, axis=1, keepdims=True)
    metabuf[my_z] = msend[...]
    pl.semaphore_wait(barrier, len(peers))

    def z_start(k):
        for j in range(1, NZ):
            z_copy(k, j).start()
        zbuf[k, my_z] = tok[:, cols(k)]

    for j in range(1, NZ):
        meta_copy(j).start()
    z_start(0)
    z_start(1)
    for copy in local:
        copy.start()
    fresh[half] = newlat[...]

    gacc[...] = jnp.zeros_like(gacc)
    uacc[...] = jnp.zeros_like(uacc)
    XS = NX * S
    c_row, p_col = iota((R, XS), 1), iota((R, XS), 0)
    place = (c_row // S) * (NZ * CAP) + ((c_row % S) // PAD) * CAP + c_row % PAD
    pmat[...] = jnp.where((place == p_col) & (c_row % PAD < CAP), 1.0, 0.0).astype(BF16)
    c_row, p_col = iota((XS, R), 0), iota((XS, R), 1)
    place = (c_row // S) * (NZ * CAP) + ((c_row % S) // PAD) * CAP + c_row % PAD
    emat[...] = jnp.where((place == p_col) & (c_row % PAD < CAP), 1.0, 0.0).astype(BF16)

    request = (req * (NX * NZ) + ep) // 2
    nodes = parents.shape[1]
    par = parents[pl.ds(request, 1), :]
    par = jnp.concatenate([par, jnp.full((1, 128 - nodes), -1, jnp.int32)], axis=1)
    down, across = iota((128, 128), 0), iota((128, 128), 1)
    reach = jnp.where((down == across) | (down == par), 1.0, 0.0)
    for _ in range(4):
        reach = jnp.minimum(mm(reach.astype(BF16), reach.astype(BF16)), 1.0)
    vis[...] = jnp.transpose(reach)[0:2 * T]

    for j in range(1, NZ):
        meta_copy(j).wait_recv()
    L = NZ * T
    ids = jnp.concatenate([metabuf[z, 0:T] for z in range(NZ)], axis=0)
    wts = jnp.concatenate([metabuf[z, T:2 * T] for z in range(NZ)], axis=0)
    slot, line = iota((L, XS), 1), iota((L, XS), 0)
    expert = ((slot // S) * NZ + my_z).astype(F32)
    named, weight = jnp.zeros((L, XS), F32), jnp.zeros((L, XS), F32)
    for top in range(rid.shape[1]):
        hit = ids[:, top:top + 1] == expert
        named = jnp.where(hit, 1.0, named)
        weight = jnp.where(hit, wts[:, top:top + 1], weight)
    r0, r1 = iota((L, L), 0), iota((L, L), 1)
    before = jnp.where((r0 // T == r1 // T) & (r1 < r0), 1.0, 0.0).astype(BF16)
    rank = mm(before, named.astype(BF16))
    mine = (named > 0.5) & ((slot % S) // PAD == line // T) & (rank == (slot % PAD).astype(F32))
    smat[...] = jnp.transpose(jnp.where(mine, 1.0, 0.0)).astype(BF16)
    weight = jnp.where(mine, weight, 0.0)
    high = weight.astype(BF16)
    whi[...] = high
    wlo[...] = (weight - high.astype(F32)).astype(BF16)

    def select(k):
        for j in range(1, NZ):
            z_copy(k, j).wait_recv()
        rows = jnp.concatenate([zbuf[k, z].astype(F32) for z in range(NZ)], axis=0).astype(BF16)
        picked = mm(smat[...], rows).astype(BF16)
        for x in range(NX):
            xsend[k, x] = picked[x * S:(x + 1) * S]
        for j in range(1, NX):
            x_copy(k, j).start()
        xbuf[k, my_x] = xsend[k, my_x]

    def gather_own(k):
        for j in range(1, NX):
            x_copy(k, j).wait_recv()
        rows = jnp.concatenate([xbuf[k, x] for x in range(NX)], axis=0)
        ybuf[k, blk_of(my_y)] = mm(pmat[...], rows).astype(BF16)
        y_copy(k, 0).start()
        y_copy(k, 1).start()
        s_copy(k, 0).start()

    def gather_near(k):
        y_copy(k, 0).wait_recv()
        y_copy(k, 2).start()
        s_copy(k, 1).start()
        y_copy(k, 1).wait_recv()
        y_copy(k, 3).start()
        s_copy(k, 2).start()

    def gather_far(k):
        y_copy(k, 2).wait_recv()
        y_copy(k, 3).wait_recv()
        s_copy(k, 3).start()

    def multiply_up(k):
        for i in range(4):
            s_copy(k, i).wait_recv()
        w_rows = pl.ds(pl.multiple_of(k * C, 128), C)

        def rows_of(i, _):
            rows = ybuf[k, pl.ds(2 * i, 2)].reshape(2 * R, C)
            at = pl.ds(pl.multiple_of(i * 2 * R, 8), 2 * R)
            gacc[at] += mm(rows, wg[w_rows])
            uacc[at] += mm(rows, wu[w_rows])
            return 0

        lax.fori_loop(0, NC * NY // 2, rows_of, 0)

    heads = qbuf.shape[1]
    ctx = cachebuf.shape[0] * cachebuf.shape[1]
    length = clen[request]

    def attend(i):
        q = qbuf[pl.ds(2 * i, 2)].reshape(2 * heads, qbuf.shape[2])
        keys = cachebuf[...].reshape(ctx, cachebuf.shape[2])
        near = jnp.concatenate([fresh[0].astype(F32), fresh[1].astype(F32)], axis=0).astype(BF16)
        s_far = mm_nt(q, keys) * score_scale
        s_near = mm_nt(q, near) * score_scale
        s_far = jnp.where(iota((2 * heads, ctx), 1) < length, s_far, -jnp.inf)
        seen = jnp.concatenate(
            [
                jnp.broadcast_to(vis[pl.ds(half * T + 2 * i + n, 1), :], (heads, 128))
                for n in range(2)
            ],
            axis=0,
        )[:, :2 * T]
        s_near = jnp.where(seen > 0.5, s_near, -jnp.inf)
        top = jnp.maximum(
            jnp.max(s_far, axis=1, keepdims=True), jnp.max(s_near, axis=1, keepdims=True)
        )
        p_far, p_near = jnp.exp(s_far - top), jnp.exp(s_near - top)
        total = jnp.sum(p_far, axis=1, keepdims=True) + jnp.sum(p_near, axis=1, keepdims=True)
        p_far, p_near = (p_far / total).astype(BF16), (p_near / total).astype(BF16)
        out = mm(p_far, keys[:, :VDIM]) + mm(p_near, near[:, :VDIM])
        obuf[pl.ds(2 * i, 2)] = out.astype(BF16).reshape(2, heads, VDIM)

    pieces = T // 2
    first_piece = K + 3 - pieces - 1

    def dispatch_step(s, _):
        @pl.when(s + 2 < K)
        def _():
            z_start(s + 2)

        @pl.when(s == 1)
        def _():
            cache_copy.start()
            fresh_copy.start()

        @pl.when(s < K)
        def _():
            select(s)

        @pl.when((s >= 1) & (s < K + 1))
        def _():
            gather_own(s - 1)

        @pl.when((s >= 2) & (s < K + 2))
        def _():
            gather_near(s - 2)

        @pl.when(s == 3)
        def _():
            local[0].wait()
            local[1].wait()

        @pl.when(s == first_piece)
        def _():
            local[3].wait()
            local[4].wait()
            cache_copy.wait_recv()
            fresh_copy.wait_recv()

        @pl.when((s >= first_piece) & (s < first_piece + pieces))
        def _():
            attend(s - first_piece)

        @pl.when(s >= 3)
        def _():
            gather_far(s - 3)
            multiply_up(s - 3)

        return 0

    lax.fori_loop(0, K + 3, dispatch_step, 0)

    out_copy = pltpu.make_async_copy(obuf, attn_out, out_sem)
    out_copy.start()
    gate = gacc[...]
    act[...] = (gate / (1.0 + jnp.exp(-gate)) * uacc[...]).astype(BF16).reshape(act.shape)
    local[2].wait()

    def down_other(k):
        rows = act[1 - my_c].reshape(NY * R, FF)
        dsend[k] = mm(rows, wd[:, cols(k)]).astype(BF16).reshape(NY, R, C)
        d_copy(k).start()

    def own_rows(k, y):
        return mm(act[my_c, y], wd[:, cols(k)]) + drecv[k, y].astype(F32)

    def send_far(k):
        d_copy(k).wait_recv()
        rows = own_rows(k, far).astype(BF16)
        r1send[k, 0] = rows[:HR]
        r1_copy(k, 0).start()
        r1send[k, 1] = rows[HR:]
        r1_copy(k, 1).start()

    def send_near(k):
        r1_copy(k, 0).wait_recv()
        rows = own_rows(k, nxt)
        more = r1recv[k, 0].astype(F32)
        r2send[k, 0] = jnp.concatenate([rows[:HR] + more, rows[HR:]], axis=0).astype(BF16)
        r2_copy(k, 0).start()
        r1_copy(k, 1).wait_recv()
        rows = own_rows(k, prv)
        more = r1recv[k, 1].astype(F32)
        r2send[k, 1] = jnp.concatenate([rows[:HR], rows[HR:] + more], axis=0).astype(BF16)
        r2_copy(k, 1).start()

    def send_back(k):
        rows = own_rows(k, my_y)
        r2_copy(k, 0).wait_recv()
        r2_copy(k, 1).wait_recv()
        rows = (rows + r2recv[k, 0].astype(F32) + r2recv[k, 1].astype(F32)).astype(BF16)
        spread = mm(emat[...], rows).astype(BF16)
        for x in range(NX):
            x2send[k, x] = spread[x * S:(x + 1) * S]
        for j in range(1, NX):
            x2_copy(k, j).start()
        x2buf[k, my_x] = x2send[k, my_x]

    def weigh(k):
        for j in range(1, NX):
            x2_copy(k, j).wait_recv()
        rows = jnp.concatenate([x2buf[k, x] for x in range(NX)], axis=0)
        sums = (mm(whi[...], rows) + mm(wlo[...], rows)).astype(BF16)
        for z in range(NZ):
            z2send[k, z] = sums[z * T:(z + 1) * T]
        for j in range(1, NZ):
            z2_copy(k, j).start()
        z2buf[k, my_z] = z2send[k, my_z]

    def finish(k):
        for j in range(1, NZ):
            z2_copy(k, j).wait_recv()
        rows = z2buf[k, 0].astype(F32)
        for z in range(1, NZ):
            rows = rows + z2buf[k, z].astype(F32)
        moe_out[:, cols(k)] = rows.astype(BF16)

    def sent_dispatch(k):
        for j in range(1, NZ):
            z_copy(k, j).wait_send()
        for j in range(1, NX):
            x_copy(k, j).wait_send()
        for i in range(4):
            y_copy(k, i).wait_send()
            s_copy(k, i).wait_send()

    def sent_combine(k):
        d_copy(k).wait_send()
        for i in range(2):
            r1_copy(k, i).wait_send()
            r2_copy(k, i).wait_send()
        for j in range(1, NX):
            x2_copy(k, j).wait_send()
        for j in range(1, NZ):
            z2_copy(k, j).wait_send()

    def combine_step(s, _):
        @pl.when(s < K)
        def _():
            down_other(s)

        @pl.when((s >= 1) & (s < K + 1))
        def _():
            send_far(s - 1)
            sent_dispatch(s - 1)

        @pl.when((s >= 2) & (s < K + 2))
        def _():
            send_near(s - 2)

        @pl.when((s >= 3) & (s < K + 3))
        def _():
            send_back(s - 3)

        @pl.when((s >= 4) & (s < K + 4))
        def _():
            weigh(s - 4)

        @pl.when(s >= 5)
        def _():
            finish(s - 5)
            sent_combine(s - 5)

        return 0

    lax.fori_loop(0, K + 5, combine_step, 0)
    for j in range(1, NZ):
        meta_copy(j).wait_send()
    cache_copy.wait_send()
    fresh_copy.wait_send()
    out_copy.wait()


def body(queries, cache, newlat, parents, clen, tok, rid, rsc, wg, wu, wd):
    T, D = tok.shape
    K = CHUNKS
    C = D // K
    S, R = NZ * PAD, NX * NZ * CAP
    HR = R // 2
    heads, lat = queries.shape[1:]
    FF = wg.shape[2]
    n_rows = NC * NY * R
    vmem, dma = pltpu.VMEM, pltpu.SemaphoreType.DMA
    anyspec, vspec = pl.BlockSpec(memory_space=pl.ANY), pl.BlockSpec(memory_space=pltpu.VMEM)
    scratch = [
        vmem((D, FF), BF16), vmem((D, FF), BF16), vmem((FF, D), BF16),
        vmem((T, heads, lat), BF16), vmem((2, cache.shape[1], lat), BF16),
        vmem((2, T, lat), BF16), vmem((2 * T, 128), F32), vmem((T, heads, VDIM), BF16),
        vmem((2 * T, 128), F32), vmem((NZ, 2 * T, 128), F32),
        vmem((NX * S, NZ * T), BF16), vmem((R, NX * S), BF16), vmem((NX * S, R), BF16),
        vmem((NZ * T, NX * S), BF16), vmem((NZ * T, NX * S), BF16),
        vmem((K, NZ, T, C), BF16), vmem((K, NX, S, C), BF16), vmem((K, NX, S, C), BF16),
        vmem((K, NC * NY, R, C), BF16), vmem((n_rows, FF), F32), vmem((n_rows, FF), F32),
        vmem((NC, NY, R, FF), BF16),
        vmem((K, NY, R, C), BF16), vmem((K, NY, R, C), BF16),
        vmem((K, 2, HR, C), BF16), vmem((K, 2, HR, C), BF16),
        vmem((K, 2, R, C), BF16), vmem((K, 2, R, C), BF16),
        vmem((K, NX, S, C), BF16), vmem((K, NX, S, C), BF16),
        vmem((K, NZ, T, C), BF16), vmem((K, NZ, T, C), BF16),
        dma((5,)), dma, dma((2,)), dma((2,)), dma((NZ - 1,)), dma((NZ - 1,)),
        dma((K, NZ - 1)), dma((K, NZ - 1)), dma((K, NX - 1)), dma((K, NX - 1)),
        dma((K, 4)), dma((K, 4)), dma((K, 4)), dma((K, 4)),
        dma((K,)), dma((K,)), dma((K, 2)), dma((K, 2)), dma((K, 2)), dma((K, 2)),
        dma((K, NX - 1)), dma((K, NX - 1)), dma((K, NZ - 1)), dma((K, NZ - 1)),
    ]
    flops = 2 * n_rows * D * FF * 3 + 2 * T * heads * 2 * cache.shape[1] * (lat + VDIM)
    return tuple(pl.pallas_call(
        kernel,
        out_shape=(
            jax.ShapeDtypeStruct((T, heads, VDIM), BF16),
            jax.ShapeDtypeStruct((T, D), BF16),
        ),
        in_specs=[
            vspec, vspec, vspec, anyspec, anyspec, vspec, vspec,
            pl.BlockSpec(memory_space=pltpu.SMEM), anyspec, anyspec, anyspec,
        ],
        out_specs=(anyspec, vspec),
        scratch_shapes=scratch,
        compiler_params=pltpu.CompilerParams(
            collective_id=0, has_side_effects=True, vmem_limit_bytes=63 * 1024 * 1024
        ),
        cost_estimate=pl.CostEstimate(flops=flops, bytes_accessed=14_000_000, transcendentals=0),
        name="verify_layer",
    )(tok, rid, rsc, queries, cache, newlat, parents, clen, wg, wu, wd))


def solution(mesh):
    placed = (
        P(("req", "ep"), None, None),
        P(("req", "ep"), None, None),
        P(("req", "ep"), None),
        P(),
        P(),
        P(("req", "ep"), None),
        P(("req", "ep"), None),
        P(("req", "ep"), None),
        P("ep", None, "req"),
        P("ep", None, "req"),
        P("ep", "req", None),
    )
    return jax.shard_map(
        body,
        mesh=mesh,
        in_specs=placed,
        out_specs=(P(("req", "ep"), None, None), P(("req", "ep"), None)),
        check_vma=False,
    )
```

time: 300 us -> 153 us (0.51)
  Pallas kernels: 0 us -> 145 us
  waiting for transfers between devices: 144 us -> 0 us
  blocking collectives: 53.2 us -> 0 us
  matrix products: 35.4 us -> 0 us
  local copies, waits for them, and re-layouts: 34.1 us -> 7 us
  between operations: 14.4 us -> 0.64 us
  starting transfers between devices: 11.8 us -> 0 us
  other arithmetic: 5.09 us -> 0 us
    pallas_call x0 -> x1, Pallas kernels: none -> 145 us  [body(): pl.pallas_call(kernel, out_shape=(jax.ShapeDtypeStruct((T, heads, VDIM),...]
    all_gather x1 -> x0, waiting for transfers between devices: 64.9 us -> none  [body(): lax.all_gather(arrived.reshape(ep_count * capacity, model_width), 'req',...]
    all_to_all x1 -> x0, blocking collectives: 53.2 us -> none  [body(): lax.all_to_all(outgoing, 'ep', split_axis=0, concat_axis=0, tiled=True)]
    reduce_scatter x1 -> x0, waiting for transfers between devices: 52.1 us -> none  [body(): lax.psum_scatter(partial_value.astype(jnp.float32).astype(jnp.bfloat16),...]
    dot_general x6 -> x0, matrix products: 35.4 us -> none  [the longest x1 18.9 us: expert_mlp(): jnp.dot(hidden, w_down[0], preferred_element_type=jnp.float32)]
    all_to_all x1 -> x0, waiting for transfers between devices: 27.1 us -> none  [body(): lax.all_to_all(summed.astype(jnp.bfloat16), 'ep', split_axis=0, concat_ax...]
    gather x16 -> x0, local copies, waits for them, and re-layouts: 10.5 us -> none  [ancestor_table(): current = parent_row[current]]
    all_to_all x1 -> x0, starting transfers between devices: 9.79 us -> none  [body(): lax.all_to_all(summed.astype(jnp.bfloat16), 'ep', split_axis=0, concat_ax...]
  transfers between devices with their start and end apart: 5 -> 0, of which waited for: 3 -> 0; matrix products, arithmetic and copies ran while one was open for 11% -> 0% of each run, Pallas kernels for 0% -> 0%
where the time goes in v1:
time: 153 us
  Pallas kernels  145 us (95%)
  local copies, waits for them, and re-layouts  7 us (5%)
    pallas_call x1, Pallas kernels, body(): pl.pallas_call(kernel, out_shape=(jax.ShapeDtypeStruct((T, heads, VDIM),...  145 us
    unnamed x4, local copies, waits for them, and re-layouts  7 us

profile of v1, /device:TPU:1, one launch (start us, length us, event | category | flops | bytes accessed | tf_op | source)
XLA Modules:
  0.0 153.1 jit_solution(7784777477590832390)
XLA Ops:
  0.6 1.4 copy.14.parents
  2.1 2.2 %copy.13.cache = bf16[1,512,576]{2,1,0:T(8,128)(2,1)} copy(bf16[1,512,576]{1,2,0:T(8,128)(2,1)} %param.12) | data formatting | bytes 1179648 | tf_op args[1]
  4.2 145.5 %verify_layer.1 = (bf16[8,64,512]{2,1,0:T(8,128)(2,1)}, bf16[8,7168]{1,0:T(8,128)(2,1)}) custom-call(bf16[8,7168]{1,0:T(8,128)(2,1)} %tok.1, s32[8,8]{1,0:T(8,128)} %rid.1, f32[8,8]{1,0:T(8,128)} %rsc.1, bf16[8,64,576]{2,1,0:T(8,128)(2,1)} %queries.1, bf16[1,512,576]{2,1,0:T(8,128)(2,1)} %copy.13.cache, bf16[8,576]{1,0:T(8,128)(2,1)} %newlat.1, ...), custom_call_target="tpu_custom_call" | custom-call | flops 9596567552 | bytes 14000000 | tf_op jit(solution)/shard_map/verify_layer/pallas_call | solution.py:477
  149.7 1.9 %copy.17 = bf16[8,64,512]{2,1,0:T(8,128)(2,1)} copy(bf16[8,64,512]{2,1,0:T(8,128)(2,1)} %get-tuple-element.4) | data formatting | bytes 1048576
  151.6 1.6 %copy.18 = bf16[8,7168]{1,0:T(8,128)(2,1)} copy(bf16[8,7168]{1,0:T(8,128)(2,1)} %get-tuple-element.5) | data formatting | bytes 229376

commit v2 on v1

v2 whole, which is shorter than its diff:
```python
import functools

import jax
import jax.numpy as jnp
from jax import lax
from jax.experimental import pallas as pl
from jax.experimental.pallas import tpu as pltpu
from jax.sharding import PartitionSpec as P

VDIM = 512
NX, NZ, NY, NC = 4, 8, 4, 2
CAP = 3
PAD = 4
CHUNKS = 7
LEAD, NEAR, FAR = 2, 2, 3
COMB_FAR, COMB_NEAR, COMB_BACK, COMB_WEIGH, COMB_END = 1, 2, 3, 4, 5
CACHE_AT, ATTEND_AT = 5, 3

score_scale = 192.0 ** (-0.5)
route_scale = 2.5
F32, BF16 = jnp.float32, jnp.bfloat16
MESH = pl.DeviceIdType.MESH


def iota(shape, dim):
    return lax.broadcasted_iota(jnp.int32, shape, dim)


def mm(a, b):
    return jnp.dot(a, b, preferred_element_type=F32)


def mm_nt(a, b):
    return lax.dot_general(a, b, (((1,), (1,)), ((), ())), preferred_element_type=F32)


def kernel(
    tok, rid, rsc, queries, cache, newlat, parents, clen, wg_h, wu_h, wd_h,
    attn_out, moe_out,
    wg, wu, wd, qbuf, cachebuf, fresh, vis, obuf,
    msend, metabuf, smat, pmat, emat, whi, wlo,
    zbuf, xsend, xbuf, ybuf, gacc, uacc, act,
    dsend, drecv, r1send, r1recv, r2send, r2recv, x2send, x2buf, z2send, z2buf,
    loc_sem, out_sem, c_send, c_recv, m_send, m_recv,
    z_send, z_recv, x_send, x_recv, y_send, y_recv, s_send, s_recv,
    d_send, d_recv, r1_send, r1_recv, r2_send, r2_recv, x2_send, x2_recv, z2_send, z2_recv,
):
    req, ep = lax.axis_index("req"), lax.axis_index("ep")
    my_y, my_c = req // NC, req % NC
    my_x, my_z = ep // NZ, ep % NZ
    K = CHUNKS
    T = tok.shape[0]
    C = tok.shape[1] // K
    S = NZ * PAD
    R = NX * NZ * CAP
    HR = R // 2
    FF = wg.shape[1]
    rot = lambda a, j, n: lax.rem(a + j + n, n)
    nxt, prv, far = rot(my_y, 1, NY), rot(my_y, -1, NY), rot(my_y, 2, NY)
    dev_y = lambda y: (y * NC + my_c, ep)
    dev_x = lambda x: (req, x * NZ + my_z)
    dev_z = lambda z: (req, my_x * NZ + z)
    sib = (my_y * NC + (1 - my_c), ep)
    blk_of = lambda y: my_c * NY + y
    half = ep % 2
    mate = (req, ep + 1 - 2 * half)
    cols = lambda k: pl.ds(pl.multiple_of(k * C, 128), C)

    def remote(src, dst, ssem, rsem, device):
        return pltpu.make_async_remote_copy(
            src_ref=src, dst_ref=dst, send_sem=ssem, recv_sem=rsem,
            device_id=device, device_id_type=MESH,
        )

    def meta_copy(j):
        return remote(msend, metabuf.at[my_z], m_send, m_recv,
                      dev_z(rot(my_z, j, NZ)))

    def z_copy(k, j):
        return remote(tok.at[:, cols(k)], zbuf.at[k, my_z], z_send,
                      z_recv.at[k], dev_z(rot(my_z, j, NZ)))

    def x_copy(k, j):
        to = rot(my_x, j, NX)
        return remote(xsend.at[k, to], xbuf.at[k, my_x], x_send,
                      x_recv.at[k], dev_x(to))

    def y_copy(k, i):
        if i < 2:
            ref = ybuf.at[k, blk_of(my_y)]
        elif i == 2:
            ref = ybuf.at[k, blk_of(prv), pl.ds(0, HR)]
        else:
            ref = ybuf.at[k, blk_of(nxt), pl.ds(HR, HR)]
        return remote(ref, ref, y_send, y_recv.at[k, i // 2],
                      dev_y(nxt if i % 2 == 0 else prv))

    def s_copy(k, i):
        ref = ybuf.at[k, blk_of((my_y, prv, nxt, far)[i])]
        return remote(ref, ref, s_send, s_recv.at[k], sib)

    def d_copy(k, i):
        part = pl.ds(0, 1) if i == 0 else pl.ds(1, NY - 1)
        return remote(dsend.at[k, part], drecv.at[k, part], d_send, d_recv.at[k, i], sib)

    def r1_copy(k, i):
        return remote(r1send.at[k, i], r1recv.at[k, i], r1_send, r1_recv.at[k],
                      dev_y(nxt if i == 0 else prv))

    def r2_copy(k, i):
        return remote(r2send.at[k, i], r2recv.at[k, i], r2_send, r2_recv.at[k],
                      dev_y(nxt if i == 0 else prv))

    def x2_copy(k, j):
        to = rot(my_x, j, NX)
        return remote(x2send.at[k, to], x2buf.at[k, my_x], x2_send,
                      x2_recv.at[k], dev_x(to))

    def z2_copy(k, j):
        to = rot(my_z, j, NZ)
        return remote(z2send.at[k, to], z2buf.at[k, my_z], z2_send,
                      z2_recv.at[k], dev_z(to))

    def bytes_of(ref, sem):
        pltpu.make_async_copy(ref, ref, sem).wait()

    cache_copy = remote(cache.at[0], cachebuf.at[half], c_send.at[0], c_recv.at[0], mate)
    fresh_copy = remote(newlat, fresh.at[half], c_send.at[1], c_recv.at[1], mate)
    local = [
        pltpu.make_async_copy(wg_h.at[0], wg, loc_sem.at[0]),
        pltpu.make_async_copy(wu_h.at[0], wu, loc_sem.at[1]),
        pltpu.make_async_copy(wd_h.at[0], wd, loc_sem.at[2]),
        pltpu.make_async_copy(queries, qbuf, loc_sem.at[3]),
        pltpu.make_async_copy(cache.at[0], cachebuf.at[half], loc_sem.at[4]),
    ]

    barrier = pltpu.get_barrier_semaphore()
    peers = [dev_z(rot(my_z, j, NZ)) for j in range(1, NZ)]
    peers += [dev_x(rot(my_x, j, NX)) for j in range(1, NX)]
    peers += [dev_y(nxt), dev_y(prv), sib]
    for peer in peers:
        pl.semaphore_signal(barrier, inc=1, device_id=peer, device_id_type=MESH)
    msend[...] = jnp.zeros_like(msend)
    msend[0:T, 0:rid.shape[1]] = rid[...].astype(F32)
    scores = rsc[...]
    msend[T:2 * T, 0:rid.shape[1]] = route_scale * scores / jnp.sum(scores, axis=1, keepdims=True)
    metabuf[my_z] = msend[...]
    for copy in local:
        copy.start()
    fresh[half] = newlat[...]
    XS = NX * S
    c_row, p_col = iota((R, XS), 1), iota((R, XS), 0)
    place = (c_row // S) * (NZ * CAP) + ((c_row % S) // PAD) * CAP + c_row % PAD
    pmat[...] = jnp.where((place == p_col) & (c_row % PAD < CAP), 1.0, 0.0).astype(BF16)
    pl.semaphore_wait(barrier, len(peers))

    def z_start(k):
        for j in range(1, NZ):
            z_copy(k, j).start()
        zbuf[k, my_z] = tok[:, cols(k)]

    for j in range(1, NZ):
        meta_copy(j).start()
    for k in range(LEAD):
        z_start(k)

    bytes_of(metabuf.at[pl.ds(0, NZ - 1)], m_recv)
    L = NZ * T
    ids = jnp.concatenate([metabuf[z, 0:T] for z in range(NZ)], axis=0)
    wts = jnp.concatenate([metabuf[z, T:2 * T] for z in range(NZ)], axis=0)
    slot, line = iota((L, XS), 1), iota((L, XS), 0)
    expert = ((slot // S) * NZ + my_z).astype(F32)
    named, weight = jnp.zeros((L, XS), F32), jnp.zeros((L, XS), F32)
    for top in range(rid.shape[1]):
        hit = ids[:, top:top + 1] == expert
        named = jnp.where(hit, 1.0, named)
        weight = jnp.where(hit, wts[:, top:top + 1], weight)
    r0, r1 = iota((L, L), 0), iota((L, L), 1)
    before = jnp.where((r0 // T == r1 // T) & (r1 < r0), 1.0, 0.0).astype(BF16)
    rank = mm(before, named.astype(BF16))
    mine = (named > 0.5) & ((slot % S) // PAD == line // T) & (rank == (slot % PAD).astype(F32))
    smat[...] = jnp.transpose(jnp.where(mine, 1.0, 0.0)).astype(BF16)
    weight = jnp.where(mine, weight, 0.0)
    high = weight.astype(BF16)
    whi[...] = high
    wlo[...] = (weight - high.astype(F32)).astype(BF16)

    def select(k):
        bytes_of(zbuf.at[k, pl.ds(0, NZ - 1)], z_recv.at[k])
        rows = jnp.concatenate([zbuf[k, z].astype(F32) for z in range(NZ)], axis=0).astype(BF16)
        picked = mm(smat[...], rows).astype(BF16)
        for x in range(NX):
            xsend[k, x] = picked[x * S:(x + 1) * S]
        for j in range(1, NX):
            x_copy(k, j).start()
        xbuf[k, my_x] = xsend[k, my_x]

    def gather_own(k):
        bytes_of(xbuf.at[k, pl.ds(0, NX - 1)], x_recv.at[k])
        rows = jnp.concatenate([xbuf[k, x] for x in range(NX)], axis=0)
        ybuf[k, blk_of(my_y)] = mm(pmat[...], rows).astype(BF16)
        y_copy(k, 0).start()
        y_copy(k, 1).start()
        s_copy(k, 0).start()

    def gather_near(k):
        bytes_of(ybuf.at[k, pl.ds(0, 2)], y_recv.at[k, 0])
        y_copy(k, 2).start()
        s_copy(k, 1).start()
        y_copy(k, 3).start()
        s_copy(k, 2).start()

    def gather_far(k):
        bytes_of(ybuf.at[k, 0], y_recv.at[k, 1])
        s_copy(k, 3).start()

    def multiply_up(k):
        bytes_of(ybuf.at[k, pl.ds(0, NY)], s_recv.at[k])
        w_rows = pl.ds(pl.multiple_of(k * C, 128), C)

        def rows_of(i, _):
            rows = ybuf[k, pl.ds(2 * i, 2)].reshape(2 * R, C)
            at = pl.ds(pl.multiple_of(i * 2 * R, 8), 2 * R)
            gacc[at] += mm(rows, wg[w_rows])
            uacc[at] += mm(rows, wu[w_rows])
            return 0

        lax.fori_loop(0, NC * NY // 2, rows_of, 0)

    request = (req * (NX * NZ) + ep) // 2
    heads = qbuf.shape[1]
    ctx = cachebuf.shape[2]

    def attend(i):
        q = qbuf[pl.ds(2 * i, 2)].reshape(2 * heads, qbuf.shape[2])
        near = jnp.concatenate([fresh[0].astype(F32), fresh[1].astype(F32)], axis=0).astype(BF16)
        held = []
        for h in range(2):
            part = mm(q, cachebuf[h]) * score_scale
            held.append(jnp.where(iota((2 * heads, ctx), 1) + h * ctx < clen[request], part, -jnp.inf))
        s_near = mm_nt(q, near) * score_scale
        seen = jnp.concatenate(
            [
                jnp.broadcast_to(vis[pl.ds(half * T + 2 * i + n, 1), :], (heads, 128))
                for n in range(2)
            ],
            axis=0,
        )[:, :2 * T]
        s_near = jnp.where(seen > 0.5, s_near, -jnp.inf)
        top = jnp.max(s_near, axis=1, keepdims=True)
        for part in held:
            top = jnp.maximum(top, jnp.max(part, axis=1, keepdims=True))
        p_near = jnp.exp(s_near - top)
        held = [jnp.exp(part - top) for part in held]
        total = jnp.sum(p_near, axis=1, keepdims=True)
        for part in held:
            total = total + jnp.sum(part, axis=1, keepdims=True)
        out = mm((p_near / total).astype(BF16), near[:, :VDIM])
        for h in range(2):
            out = out + mm_nt((held[h] / total).astype(BF16), cachebuf[h, 0:VDIM, :])
        obuf[pl.ds(2 * i, 2)] = out.astype(BF16).reshape(2, heads, VDIM)

    pieces = T // 2

    def dispatch_step(s, _):
        @pl.when(s + LEAD < K)
        def _():
            z_start(s + LEAD)

        @pl.when(s == CACHE_AT)
        def _():
            cache_copy.start()
            fresh_copy.start()

        @pl.when(s < K)
        def _():
            select(s)

        @pl.when(s == 0)
        def _():
            gacc[...] = jnp.zeros_like(gacc)
            uacc[...] = jnp.zeros_like(uacc)

        @pl.when((s >= 1) & (s < K + 1))
        def _():
            gather_own(s - 1)

        @pl.when((s >= NEAR) & (s < K + NEAR))
        def _():
            gather_near(s - NEAR)

        @pl.when(s == FAR)
        def _():
            local[0].wait()
            local[1].wait()

        @pl.when(s >= FAR)
        def _():
            gather_far(s - FAR)
            multiply_up(s - FAR)

        return 0

    lax.fori_loop(0, K + FAR, dispatch_step, 0)

    for i, core in enumerate((my_c, 1 - my_c)):
        for n, y in enumerate((far, nxt, prv, my_y)):
            at = pl.ds(pl.multiple_of((core * NY + y) * R, 8), R)
            gate = gacc[at]
            act[i, n] = (gate / (1.0 + jnp.exp(-gate)) * uacc[at]).astype(BF16)
    local[2].wait()

    def down_other(k):
        dsend[k, 0] = mm(act[1, 0], wd[:, cols(k)]).astype(BF16)
        d_copy(k, 0).start()
        rows = act[1, 1:NY].reshape((NY - 1) * R, FF)
        dsend[k, pl.ds(1, NY - 1)] = mm(rows, wd[:, cols(k)]).astype(BF16).reshape(NY - 1, R, C)
        d_copy(k, 1).start()

    def own_rows(k, n):
        return mm(act[0, n], wd[:, cols(k)]) + drecv[k, n].astype(F32)

    def send_far(k):
        d_copy(k, 0).wait_recv()
        rows = own_rows(k, 0).astype(BF16)
        r1send[k, 0] = rows[:HR]
        r1_copy(k, 0).start()
        r1send[k, 1] = rows[HR:]
        r1_copy(k, 1).start()

    def send_near(k):
        d_copy(k, 1).wait_recv()
        rows = own_rows(k, 1)
        bytes_of(r1recv.at[k], r1_recv.at[k])
        more = r1recv[k, 0].astype(F32)
        r2send[k, 0] = jnp.concatenate([rows[:HR] + more, rows[HR:]], axis=0).astype(BF16)
        r2_copy(k, 0).start()
        rows = own_rows(k, 2)
        more = r1recv[k, 1].astype(F32)
        r2send[k, 1] = jnp.concatenate([rows[:HR], rows[HR:] + more], axis=0).astype(BF16)
        r2_copy(k, 1).start()

    def send_back(k):
        rows = own_rows(k, 3)
        bytes_of(r2recv.at[k], r2_recv.at[k])
        rows = (rows + r2recv[k, 0].astype(F32) + r2recv[k, 1].astype(F32)).astype(BF16)
        spread = mm(emat[...], rows).astype(BF16)
        for x in range(NX):
            x2send[k, x] = spread[x * S:(x + 1) * S]
        for j in range(1, NX):
            x2_copy(k, j).start()
        x2buf[k, my_x] = x2send[k, my_x]

    def weigh(k):
        bytes_of(x2buf.at[k, pl.ds(0, NX - 1)], x2_recv.at[k])
        rows = jnp.concatenate([x2buf[k, x] for x in range(NX)], axis=0)
        sums = (mm(whi[...], rows) + mm(wlo[...], rows)).astype(BF16)
        for z in range(NZ):
            z2send[k, z] = sums[z * T:(z + 1) * T]
        for j in range(1, NZ):
            z2_copy(k, j).start()
        z2buf[k, my_z] = z2send[k, my_z]

    def finish(k):
        bytes_of(z2buf.at[k, pl.ds(0, NZ - 1)], z2_recv.at[k])
        rows = z2buf[k, 0].astype(F32)
        for z in range(1, NZ):
            rows = rows + z2buf[k, z].astype(F32)
        moe_out[:, cols(k)] = rows.astype(BF16)

    def tables():
        c_row, p_col = iota((XS, R), 0), iota((XS, R), 1)
        place = (c_row // S) * (NZ * CAP) + ((c_row % S) // PAD) * CAP + c_row % PAD
        emat[...] = jnp.where((place == p_col) & (c_row % PAD < CAP), 1.0, 0.0).astype(BF16)


        nodes = parents.shape[0]
        pick = iota(parents.shape, 1) == request
        par = jnp.sum(jnp.where(pick, parents[...], 0), axis=1, keepdims=True)
        par = jnp.concatenate([par, jnp.full((128 - nodes, 1), -1, jnp.int32)], axis=0)
        down, across = iota((128, 128), 0), iota((128, 128), 1)
        reach = jnp.where((down == across) | (across == par), 1.0, 0.0)
        for _ in range(4):
            reach = jnp.minimum(mm(reach.astype(BF16), reach.astype(BF16)), 1.0)
        vis[...] = reach[0:2 * T]

    def combine_step(s, _):
        @pl.when(s < K)
        def _():
            down_other(s)

        @pl.when((s >= COMB_FAR) & (s < K + COMB_FAR))
        def _():
            send_far(s - COMB_FAR)

        @pl.when(s == COMB_FAR)
        def _():
            tables()

        @pl.when((s >= COMB_NEAR) & (s < K + COMB_NEAR))
        def _():
            send_near(s - COMB_NEAR)

        @pl.when(s == ATTEND_AT)
        def _():
            local[3].wait()
            local[4].wait()
            cache_copy.wait_recv()
            fresh_copy.wait_recv()

        @pl.when((s >= COMB_BACK) & (s < K + COMB_BACK))
        def _():
            send_back(s - COMB_BACK)

        @pl.when((s >= ATTEND_AT) & (s < ATTEND_AT + pieces))
        def _():
            attend(s - ATTEND_AT)

        @pl.when(s == ATTEND_AT + pieces)
        def _():
            out_copy.start()

        @pl.when((s >= COMB_WEIGH) & (s < K + COMB_WEIGH))
        def _():
            weigh(s - COMB_WEIGH)

        @pl.when(s >= COMB_END)
        def _():
            finish(s - COMB_END)

        return 0

    out_copy = pltpu.make_async_copy(obuf, attn_out, out_sem)
    lax.fori_loop(0, K + COMB_END, combine_step, 0)
    bytes_of(metabuf.at[pl.ds(0, NZ - 1)], m_send)
    bytes_of(zbuf.at[:, pl.ds(0, NZ - 1)], z_send)
    bytes_of(xbuf.at[:, pl.ds(0, NX - 1)], x_send)
    bytes_of(ybuf.at[:, pl.ds(0, 3)], y_send)
    bytes_of(ybuf.at[:, pl.ds(0, NY)], s_send)
    bytes_of(drecv, d_send)
    bytes_of(r1recv, r1_send)
    bytes_of(r2recv, r2_send)
    bytes_of(x2buf.at[:, pl.ds(0, NX - 1)], x2_send)
    bytes_of(z2buf.at[:, pl.ds(0, NZ - 1)], z2_send)
    cache_copy.wait_send()
    fresh_copy.wait_send()
    out_copy.wait()


def body(queries, cache, newlat, parents, clen, tok, rid, rsc, wg, wu, wd):
    cache, parents = jnp.swapaxes(cache, 1, 2), parents.T
    T, D = tok.shape
    K = CHUNKS
    C = D // K
    S, R = NZ * PAD, NX * NZ * CAP
    HR = R // 2
    heads, lat = queries.shape[1:]
    FF = wg.shape[2]
    n_rows = NC * NY * R
    vmem, dma = pltpu.VMEM, pltpu.SemaphoreType.DMA
    anyspec, vspec = pl.BlockSpec(memory_space=pl.ANY), pl.BlockSpec(memory_space=pltpu.VMEM)
    scratch = [
        vmem((D, FF), BF16), vmem((D, FF), BF16), vmem((FF, D), BF16),
        vmem((T, heads, lat), BF16), vmem((2, lat, cache.shape[2]), BF16),
        vmem((2, T, lat), BF16), vmem((2 * T, 128), F32), vmem((T, heads, VDIM), BF16),
        vmem((2 * T, 128), F32), vmem((NZ, 2 * T, 128), F32),
        vmem((NX * S, NZ * T), BF16), vmem((R, NX * S), BF16), vmem((NX * S, R), BF16),
        vmem((NZ * T, NX * S), BF16), vmem((NZ * T, NX * S), BF16),
        vmem((K, NZ, T, C), BF16), vmem((K, NX, S, C), BF16), vmem((K, NX, S, C), BF16),
        vmem((K, NC * NY, R, C), BF16), vmem((n_rows, FF), F32), vmem((n_rows, FF), F32),
        vmem((NC, NY, R, FF), BF16),
        vmem((K, NY, R, C), BF16), vmem((K, NY, R, C), BF16),
        vmem((K, 2, HR, C), BF16), vmem((K, 2, HR, C), BF16),
        vmem((K, 2, R, C), BF16), vmem((K, 2, R, C), BF16),
        vmem((K, NX, S, C), BF16), vmem((K, NX, S, C), BF16),
        vmem((K, NZ, T, C), BF16), vmem((K, NZ, T, C), BF16),
        dma((5,)), dma, dma((2,)), dma((2,)), dma, dma,
        dma, dma((K,)), dma, dma((K,)), dma, dma((K, 2)), dma, dma((K,)),
        dma, dma((K, 2)), dma, dma((K,)), dma, dma((K,)), dma, dma((K,)), dma, dma((K,)),
    ]
    flops = 2 * n_rows * D * FF * 3 + 2 * T * heads * 2 * cache.shape[2] * (lat + VDIM)
    return tuple(pl.pallas_call(
        kernel,
        out_shape=(
            jax.ShapeDtypeStruct((T, heads, VDIM), BF16),
            jax.ShapeDtypeStruct((T, D), BF16),
        ),
        in_specs=[
            vspec, vspec, vspec, anyspec, anyspec, vspec, vspec,
            pl.BlockSpec(memory_space=pltpu.SMEM), anyspec, anyspec, anyspec,
        ],
        out_specs=(anyspec, vspec),
        scratch_shapes=scratch,
        compiler_params=pltpu.CompilerParams(
            collective_id=0, has_side_effects=True, vmem_limit_bytes=63 * 1024 * 1024
        ),
        cost_estimate=pl.CostEstimate(flops=flops, bytes_accessed=14_000_000, transcendentals=0),
        name="verify_layer",
    )(tok, rid, rsc, queries, cache, newlat, parents, clen, wg, wu, wd))


def solution(mesh):
    placed = (
        P(("req", "ep"), None, None),
        P(("req", "ep"), None, None),
        P(("req", "ep"), None),
        P(),
        P(),
        P(("req", "ep"), None),
        P(("req", "ep"), None),
        P(("req", "ep"), None),
        P("ep", None, "req"),
        P("ep", None, "req"),
        P("ep", "req", None),
    )
    return jax.shard_map(
        body,
        mesh=mesh,
        in_specs=placed,
        out_specs=(P(("req", "ep"), None, None), P(("req", "ep"), None)),
        check_vma=False,
    )
```

time: 153 us -> 140 us (0.915)
  Pallas kernels: 145 us -> 136 us
  local copies, waits for them, and re-layouts: 7 us -> 3.42 us
    pallas_call x1, Pallas kernels: 145 us -> 136 us  [body(): pl.pallas_call(kernel, out_shape=(jax.ShapeDtypeStruct((T, heads, VDIM),...]
    unnamed x4 -> x2, local copies, waits for them, and re-layouts: 7 us -> 3.42 us
where the time goes in v2:
time: 140 us
  Pallas kernels  136 us (97%)
  local copies, waits for them, and re-layouts  3.42 us (2%)
    pallas_call x1, Pallas kernels, body(): pl.pallas_call(kernel, out_shape=(jax.ShapeDtypeStruct((T, heads, VDIM),...  136 us
    unnamed x2, local copies, waits for them, and re-layouts  3.42 us

profile of v2, /device:TPU:1, one launch (start us, length us, event | category | flops | bytes accessed | tf_op | source)
XLA Modules:
  0.0 139.6 jit_solution(16908490254360806020)
XLA Ops:
  0.6 135.6 %verify_layer.1 = (bf16[8,64,512]{2,1,0:T(8,128)(2,1)}, bf16[8,7168]{1,0:T(8,128)(2,1)}) custom-call(bf16[8,7168]{1,0:T(8,128)(2,1)} %tok.1, s32[8,8]{1,0:T(8,128)} %rid.1, f32[8,8]{1,0:T(8,128)} %rsc.1, bf16[8,64,576]{2,1,0:T(8,128)(2,1)} %queries.1, bf16[1,576,512]{2,1,0:T(8,128)(2,1)} %bitcast.2, bf16[8,576]{1,0:T(8,128)(2,1)} %newlat.1, ...), custom_call_target="tpu_custom_call" | custom-call | flops 9596567552 | bytes 14000000 | tf_op jit(solution)/shard_map/verify_layer/pallas_call | solution.py:482
  136.2 1.9 %copy.15 = bf16[8,64,512]{2,1,0:T(8,128)(2,1)} copy(bf16[8,64,512]{2,1,0:T(8,128)(2,1)} %get-tuple-element.4) | data formatting | bytes 1048576
  138.1 1.6 %copy.16 = bf16[8,7168]{1,0:T(8,128)(2,1)} copy(bf16[8,7168]{1,0:T(8,128)(2,1)} %get-tuple-element.5) | data formatting | bytes 229376

commit v3 on v2

--- a/solution.py
+++ b/solution.py
@@ -12,9 +12,11 @@
 CAP = 3
 PAD = 4
 CHUNKS = 7
+Z_ORDER = sorted(range(1, NZ), key=lambda j: -min(j, NZ - j))
+X_ORDER = sorted(range(1, NX), key=lambda j: -min(j, NX - j))
 LEAD, NEAR, FAR = 2, 2, 3
-COMB_FAR, COMB_NEAR, COMB_BACK, COMB_WEIGH, COMB_END = 1, 2, 3, 4, 5
-CACHE_AT, ATTEND_AT = 5, 3
+COMB_FAR, COMB_NEAR, COMB_BACK, COMB_WEIGH, COMB_END = 0, 1, 2, 3, 4
+CACHE_AT, ATTEND_AT = 5, 2
 
 score_scale = 192.0 ** (-0.5)
 route_scale = 2.5
@@ -155,11 +157,11 @@
     pl.semaphore_wait(barrier, len(peers))
 
     def z_start(k):
-        for j in range(1, NZ):
+        for j in Z_ORDER:
             z_copy(k, j).start()
         zbuf[k, my_z] = tok[:, cols(k)]
 
-    for j in range(1, NZ):
+    for j in Z_ORDER:
         meta_copy(j).start()
     for k in range(LEAD):
         z_start(k)
@@ -191,7 +193,7 @@
         picked = mm(smat[...], rows).astype(BF16)
         for x in range(NX):
             xsend[k, x] = picked[x * S:(x + 1) * S]
-        for j in range(1, NX):
+        for j in X_ORDER:
             x_copy(k, j).start()
         xbuf[k, my_x] = xsend[k, my_x]
 
@@ -215,7 +217,6 @@
         s_copy(k, 3).start()
 
     def multiply_up(k):
-        bytes_of(ybuf.at[k, pl.ds(0, NY)], s_recv.at[k])
         w_rows = pl.ds(pl.multiple_of(k * C, 128), C)
 
         def rows_of(i, _):
@@ -225,7 +226,10 @@
             uacc[at] += mm(rows, wu[w_rows])
             return 0
 
-        lax.fori_loop(0, NC * NY // 2, rows_of, 0)
+        pairs = NY // 2
+        lax.fori_loop(my_c * pairs, my_c * pairs + pairs, rows_of, 0)
+        bytes_of(ybuf.at[k, pl.ds(0, NY)], s_recv.at[k])
+        lax.fori_loop((1 - my_c) * pairs, (1 - my_c) * pairs + pairs, rows_of, 0)
 
     request = (req * (NX * NZ) + ep) // 2
     heads = qbuf.shape[1]
@@ -272,6 +276,10 @@
             cache_copy.start()
             fresh_copy.start()
 
+        @pl.when((s >= 1) & (s < K + 1))
+        def _():
+            gather_own(s - 1)
+
         @pl.when(s < K)
         def _():
             select(s)
@@ -281,10 +289,6 @@
             gacc[...] = jnp.zeros_like(gacc)
             uacc[...] = jnp.zeros_like(uacc)
 
-        @pl.when((s >= 1) & (s < K + 1))
-        def _():
-            gather_own(s - 1)
-
         @pl.when((s >= NEAR) & (s < K + NEAR))
         def _():
             gather_near(s - NEAR)
@@ -303,12 +307,11 @@
 
     lax.fori_loop(0, K + FAR, dispatch_step, 0)
 
-    for i, core in enumerate((my_c, 1 - my_c)):
+    def activate(i, core):
         for n, y in enumerate((far, nxt, prv, my_y)):
             at = pl.ds(pl.multiple_of((core * NY + y) * R, 8), R)
             gate = gacc[at]
             act[i, n] = (gate / (1.0 + jnp.exp(-gate)) * uacc[at]).astype(BF16)
-    local[2].wait()
 
     def down_other(k):
         dsend[k, 0] = mm(act[1, 0], wd[:, cols(k)]).astype(BF16)
@@ -347,7 +350,7 @@
         spread = mm(emat[...], rows).astype(BF16)
         for x in range(NX):
             x2send[k, x] = spread[x * S:(x + 1) * S]
-        for j in range(1, NX):
+        for j in X_ORDER:
             x2_copy(k, j).start()
         x2buf[k, my_x] = x2send[k, my_x]
 
@@ -357,7 +360,7 @@
         sums = (mm(whi[...], rows) + mm(wlo[...], rows)).astype(BF16)
         for z in range(NZ):
             z2send[k, z] = sums[z * T:(z + 1) * T]
-        for j in range(1, NZ):
+        for j in Z_ORDER:
             z2_copy(k, j).start()
         z2buf[k, my_z] = z2send[k, my_z]
 
@@ -385,21 +388,21 @@
         vis[...] = reach[0:2 * T]
 
     def combine_step(s, _):
-        @pl.when(s < K)
-        def _():
-            down_other(s)
-
         @pl.when((s >= COMB_FAR) & (s < K + COMB_FAR))
         def _():
             send_far(s - COMB_FAR)
 
-        @pl.when(s == COMB_FAR)
+        @pl.when(s + 1 < K)
+        def _():
+            down_other(s + 1)
+
+        @pl.when((s >= COMB_NEAR) & (s < K + COMB_NEAR))
+        def _():
+            send_near(s - COMB_NEAR)
+
+        @pl.when(s == COMB_NEAR)
         def _():
             tables()
-
-        @pl.when((s >= COMB_NEAR) & (s < K + COMB_NEAR))
-        def _():
-            send_near(s - COMB_NEAR)
 
         @pl.when(s == ATTEND_AT)
         def _():
@@ -431,6 +434,10 @@
         return 0
 
     out_copy = pltpu.make_async_copy(obuf, attn_out, out_sem)
+    activate(1, 1 - my_c)
+    local[2].wait()
+    down_other(0)
+    activate(0, my_c)
     lax.fori_loop(0, K + COMB_END, combine_step, 0)
     bytes_of(metabuf.at[pl.ds(0, NZ - 1)], m_send)
     bytes_of(zbuf.at[:, pl.ds(0, NZ - 1)], z_send)
@@ -445,6 +452,11 @@
     cache_copy.wait_send()
     fresh_copy.wait_send()
     out_copy.wait()
+
+
+def keep(attended, summed, attn_out, moe_out):
+    attn_out[...] = attended[...]
+    moe_out[...] = summed[...]
 
 
 def body(queries, cache, newlat, parents, clen, tok, rid, rsc, wg, wu, wd):
@@ -479,7 +491,7 @@
         dma, dma((K, 2)), dma, dma((K,)), dma, dma((K,)), dma, dma((K,)), dma, dma((K,)),
     ]
     flops = 2 * n_rows * D * FF * 3 + 2 * T * heads * 2 * cache.shape[2] * (lat + VDIM)
-    return tuple(pl.pallas_call(
+    attended, summed = pl.pallas_call(
         kernel,
         out_shape=(
             jax.ShapeDtypeStruct((T, heads, VDIM), BF16),
@@ -496,7 +508,16 @@
         ),
         cost_estimate=pl.CostEstimate(flops=flops, bytes_accessed=14_000_000, transcendentals=0),
         name="verify_layer",
-    )(tok, rid, rsc, queries, cache, newlat, parents, clen, wg, wu, wd))
+    )(tok, rid, rsc, queries, cache, newlat, parents, clen, wg, wu, wd)
+    return tuple(pl.pallas_call(
+        keep,
+        out_shape=(
+            jax.ShapeDtypeStruct(attended.shape, BF16), jax.ShapeDtypeStruct(summed.shape, BF16)
+        ),
+        in_specs=[vspec, vspec],
+        out_specs=(vspec, vspec),
+        name="keep_results",
+    )(attended, summed))
 
 
 def solution(mesh):

time: 140 us -> 136 us (0.971)
  local copies, waits for them, and re-layouts: 3.42 us -> 0 us
  Pallas kernels: 136 us -> 134 us
    unnamed x2 -> x0, local copies, waits for them, and re-layouts: 3.42 us -> none
    pallas_call x1, Pallas kernels: 136 us -> 132 us  [body(): pl.pallas_call(kernel, out_shape=(jax.ShapeDtypeStruct((T, heads, VDIM),...]
    pallas_call x0 -> x1, Pallas kernels: none -> 1.91 us  [body(): pl.pallas_call(keep, out_shape=(jax.ShapeDtypeStruct(attended.shape, BF16...]
where the time goes in v3:
time: 136 us; the launch traced here: 135 us
  Pallas kernels  134 us (99%)
    pallas_call x1, Pallas kernels, body(): pl.pallas_call(kernel, out_shape=(jax.ShapeDtypeStruct((T, heads, VDIM),...  132 us

profile of v3, /device:TPU:1, one launch (start us, length us, event | category | flops | bytes accessed | tf_op | source)
XLA Modules:
  0.0 135.0 jit_solution(8303858837834215486)
XLA Ops:
  0.6 132.5 %verify_layer.1 = (bf16[8,64,512]{2,1,0:T(8,128)(2,1)}, bf16[8,7168]{1,0:T(8,128)(2,1)}) custom-call(bf16[8,7168]{1,0:T(8,128)(2,1)} %tok.1, s32[8,8]{1,0:T(8,128)} %rid.1, f32[8,8]{1,0:T(8,128)} %rsc.1, bf16[8,64,576]{2,1,0:T(8,128)(2,1)} %queries.1, bf16[1,576,512]{2,1,0:T(8,128)(2,1)} %bitcast.2, bf16[8,576]{1,0:T(8,128)(2,1)} %newlat.1, ...), custom_call_target="tpu_custom_call" | custom-call | flops 9596567552 | bytes 14000000 | tf_op jit(solution)/shard_map/verify_layer/pallas_call | solution.py:494
  133.1 1.9 %keep_results.1 = (bf16[8,64,512]{2,1,0:T(8,128)(2,1)}, bf16[8,7168]{1,0:T(8,128)(2,1)}) custom-call(bf16[8,64,512]{2,1,0:T(8,128)(2,1)} %get-tuple-element.4.attended, bf16[8,7168]{1,0:T(8,128)(2,1)} %get-tuple-element.5.summed), custom_call_target="tpu_custom_call" | custom-call | tf_op jit(solution)/shard_map/keep_results/pallas_call | solution.py:512

commit v4 on v3

--- a/solution.py
+++ b/solution.py
@@ -14,7 +14,7 @@
 CHUNKS = 7
 Z_ORDER = sorted(range(1, NZ), key=lambda j: -min(j, NZ - j))
 X_ORDER = sorted(range(1, NX), key=lambda j: -min(j, NX - j))
-LEAD, NEAR, FAR = 2, 2, 3
+LEAD, NEAR, FAR = 2, 2, 4
 COMB_FAR, COMB_NEAR, COMB_BACK, COMB_WEIGH, COMB_END = 0, 1, 2, 3, 4
 CACHE_AT, ATTEND_AT = 5, 2
 
@@ -88,12 +88,8 @@
                       x_recv.at[k], dev_x(to))
 
     def y_copy(k, i):
-        if i < 2:
-            ref = ybuf.at[k, blk_of(my_y)]
-        elif i == 2:
-            ref = ybuf.at[k, blk_of(prv), pl.ds(0, HR)]
-        else:
-            ref = ybuf.at[k, blk_of(nxt), pl.ds(HR, HR)]
+        y = my_y if i < 4 else (prv, nxt)[i - 4]
+        ref = ybuf.at[k, blk_of(y), pl.ds((0, HR, HR, 0, 0, HR)[i], HR)]
         return remote(ref, ref, y_send, y_recv.at[k, i // 2],
                       dev_y(nxt if i % 2 == 0 else prv))
 
@@ -201,19 +197,20 @@
         bytes_of(xbuf.at[k, pl.ds(0, NX - 1)], x_recv.at[k])
         rows = jnp.concatenate([xbuf[k, x] for x in range(NX)], axis=0)
         ybuf[k, blk_of(my_y)] = mm(pmat[...], rows).astype(BF16)
-        y_copy(k, 0).start()
-        y_copy(k, 1).start()
+        for i in range(4):
+            y_copy(k, i).start()
         s_copy(k, 0).start()
 
     def gather_near(k):
-        bytes_of(ybuf.at[k, pl.ds(0, 2)], y_recv.at[k, 0])
-        y_copy(k, 2).start()
+        bytes_of(ybuf.at[k, 0], y_recv.at[k, 0])
+        y_copy(k, 4).start()
+        y_copy(k, 5).start()
+        bytes_of(ybuf.at[k, 0], y_recv.at[k, 1])
         s_copy(k, 1).start()
-        y_copy(k, 3).start()
         s_copy(k, 2).start()
 
     def gather_far(k):
-        bytes_of(ybuf.at[k, 0], y_recv.at[k, 1])
+        bytes_of(ybuf.at[k, 0], y_recv.at[k, 2])
         s_copy(k, 3).start()
 
     def multiply_up(k):
@@ -487,7 +484,7 @@
         vmem((K, NX, S, C), BF16), vmem((K, NX, S, C), BF16),
         vmem((K, NZ, T, C), BF16), vmem((K, NZ, T, C), BF16),
         dma((5,)), dma, dma((2,)), dma((2,)), dma, dma,
-        dma, dma((K,)), dma, dma((K,)), dma, dma((K, 2)), dma, dma((K,)),
+        dma, dma((K,)), dma, dma((K,)), dma, dma((K, 3)), dma, dma((K,)),
         dma, dma((K, 2)), dma, dma((K,)), dma, dma((K,)), dma, dma((K,)), dma, dma((K,)),
     ]
     flops = 2 * n_rows * D * FF * 3 + 2 * T * heads * 2 * cache.shape[2] * (lat + VDIM)

time: 136 us -> 135 us (level)
  no operation moved by 1% of the time
where the time goes in v4:
time: 135 us; the launch traced here: 134 us
  Pallas kernels  134 us (99%)
    pallas_call x1, Pallas kernels, body(): pl.pallas_call(kernel, out_shape=(jax.ShapeDtypeStruct((T, heads, VDIM),...  132 us

profile of v4, /device:TPU:1, one launch (start us, length us, event | category | flops | bytes accessed | tf_op | source)
XLA Modules:
  0.0 134.5 jit_solution(10207106104003738846)
XLA Ops:
  0.6 131.9 %verify_layer.1 = (bf16[8,64,512]{2,1,0:T(8,128)(2,1)}, bf16[8,7168]{1,0:T(8,128)(2,1)}) custom-call(bf16[8,7168]{1,0:T(8,128)(2,1)} %tok.1, s32[8,8]{1,0:T(8,128)} %rid.1, f32[8,8]{1,0:T(8,128)} %rsc.1, bf16[8,64,576]{2,1,0:T(8,128)(2,1)} %queries.1, bf16[1,576,512]{2,1,0:T(8,128)(2,1)} %bitcast.2, bf16[8,576]{1,0:T(8,128)(2,1)} %newlat.1, ...), custom_call_target="tpu_custom_call" | custom-call | flops 9596567552 | bytes 14000000 | tf_op jit(solution)/shard_map/verify_layer/pallas_call | solution.py:491
  132.6 1.9 %keep_results.1 = (bf16[8,64,512]{2,1,0:T(8,128)(2,1)}, bf16[8,7168]{1,0:T(8,128)(2,1)}) custom-call(bf16[8,64,512]{2,1,0:T(8,128)(2,1)} %get-tuple-element.4.attended, bf16[8,7168]{1,0:T(8,128)(2,1)} %get-tuple-element.5.summed), custom_call_target="tpu_custom_call" | custom-call | tf_op jit(solution)/shard_map/keep_results/pallas_call | solution.py:509

commit v5 on v4

--- a/solution.py
+++ b/solution.py
@@ -105,8 +105,9 @@
         return remote(r1send.at[k, i], r1recv.at[k, i], r1_send, r1_recv.at[k],
                       dev_y(nxt if i == 0 else prv))
 
-    def r2_copy(k, i):
-        return remote(r2send.at[k, i], r2recv.at[k, i], r2_send, r2_recv.at[k],
+    def r2_copy(k, i, h):
+        part = pl.ds(h * HR, HR)
+        return remote(r2send.at[k, i, part], r2recv.at[k, i, part], r2_send, r2_recv.at[k],
                       dev_y(nxt if i == 0 else prv))
 
     def x2_copy(k, j):
@@ -328,17 +329,21 @@
         r1send[k, 1] = rows[HR:]
         r1_copy(k, 1).start()
 
+        bytes_of(drecv.at[k, pl.ds(1, NY - 1)], d_recv.at[k, 1])
+        for i in range(2):
+            r2send[k, i, pl.ds((1 - i) * HR, HR)] = half_rows(k, i + 1, 1 - i).astype(BF16)
+            r2_copy(k, i, 1 - i).start()
+
+    def half_rows(k, n, h):
+        part = pl.ds(h * HR, HR)
+        return mm(act[0, n, part], wd[:, cols(k)]) + drecv[k, n, part].astype(F32)
+
     def send_near(k):
-        d_copy(k, 1).wait_recv()
-        rows = own_rows(k, 1)
         bytes_of(r1recv.at[k], r1_recv.at[k])
-        more = r1recv[k, 0].astype(F32)
-        r2send[k, 0] = jnp.concatenate([rows[:HR] + more, rows[HR:]], axis=0).astype(BF16)
-        r2_copy(k, 0).start()
-        rows = own_rows(k, 2)
-        more = r1recv[k, 1].astype(F32)
-        r2send[k, 1] = jnp.concatenate([rows[:HR], rows[HR:] + more], axis=0).astype(BF16)
-        r2_copy(k, 1).start()
+        for i in range(2):
+            rows = half_rows(k, i + 1, i) + r1recv[k, i].astype(F32)
+            r2send[k, i, pl.ds(i * HR, HR)] = rows.astype(BF16)
+            r2_copy(k, i, i).start()
 
     def send_back(k):
         rows = own_rows(k, 3)

time: 135 us -> 138 us (1.022)
  Pallas kernels: 134 us -> 137 us
    pallas_call x1, Pallas kernels: 132 us -> 135 us  [body(): pl.pallas_call(kernel, out_shape=(jax.ShapeDtypeStruct((T, heads, VDIM),...]
where the time goes in v5:
time: 138 us
  Pallas kernels  137 us (99%)
    pallas_call x1, Pallas kernels, body(): pl.pallas_call(kernel, out_shape=(jax.ShapeDtypeStruct((T, heads, VDIM),...  135 us

profile of v5, /device:TPU:1, one launch (start us, length us, event | category | flops | bytes accessed | tf_op | source)
XLA Modules:
  0.0 138.0 jit_solution(12439186178813155152)
XLA Ops:
  0.6 135.4 %verify_layer.1 = (bf16[8,64,512]{2,1,0:T(8,128)(2,1)}, bf16[8,7168]{1,0:T(8,128)(2,1)}) custom-call(bf16[8,7168]{1,0:T(8,128)(2,1)} %tok.1, s32[8,8]{1,0:T(8,128)} %rid.1, f32[8,8]{1,0:T(8,128)} %rsc.1, bf16[8,64,576]{2,1,0:T(8,128)(2,1)} %queries.1, bf16[1,576,512]{2,1,0:T(8,128)(2,1)} %bitcast.2, bf16[8,576]{1,0:T(8,128)(2,1)} %newlat.1, ...), custom_call_target="tpu_custom_call" | custom-call | flops 9596567552 | bytes 14000000 | tf_op jit(solution)/shard_map/verify_layer/pallas_call | solution.py:496
  136.0 1.9 %keep_results.1 = (bf16[8,64,512]{2,1,0:T(8,128)(2,1)}, bf16[8,7168]{1,0:T(8,128)(2,1)}) custom-call(bf16[8,64,512]{2,1,0:T(8,128)(2,1)} %get-tuple-element.4.attended, bf16[8,7168]{1,0:T(8,128)(2,1)} %get-tuple-element.5.summed), custom_call_target="tpu_custom_call" | custom-call | tf_op jit(solution)/shard_map/keep_results/pallas_call | solution.py:514
